TPU v7x, 32 devices: a whole 2x2x4 slice. The times are simulated.
32 devices in a mesh: ma: 8 (over z, x), ao: 4 (over y, core).
Axes of the slice: x: 2, y: 2, z: 4, core: 2. Of those that a mesh axis runs over, the one named last changes fastest.
Arguments:
- truth_table: bfloat16 [4, 512, 512, 128], P('ao', 'ma'), may hold values from -1 to 1, as said below
- pair_list: int32 [4], replicated, may hold values from 0 to 3, as said below
Outputs:
- cross_corr: float32 [4, 512, 512, 128], P('ao', 'ma')
Inputs may be any that keep to these rules, and one draw needn't show every extreme that they name: `truth_table`: every entry is +1 or -1. `pair_list`: each output's partner is another output, and every output is the partner of exactly one output.
All inputs are finite; a program needn't handle non-finite values.
Results may differ from a plain program's by a relative error of at most 0.0003.
Values sent between devices are 32-bit elements; how exact they have to be, the bound alone decides.
A program may use at most 192 MiB of HBM per device.

v0:
```python
import jax
import jax.numpy as jnp
from jax import lax
from jax.sharding import PartitionSpec as P


def sylvester(length):
    index_row = jnp.arange(length, dtype=jnp.int32)
    shared = jnp.bitwise_and(index_row[:, None], index_row[None, :])
    ones_count = jnp.zeros((length, length), jnp.int32)
    for position in range(length.bit_length() - 1):
        ones_count = ones_count + jnp.bitwise_and(jnp.right_shift(shared, position), 1)
    return (1 - 2 * (ones_count % 2)).astype(jnp.float32)


def apply_low(field, h_low):
    return jnp.einsum("abj,jc->abc", field, h_low, precision=lax.Precision.HIGHEST)


def apply_mid(field, h_mid):
    return jnp.einsum("bj,ajc->abc", h_mid, field, precision=lax.Precision.HIGHEST)


def apply_high(field, h_high, factor):
    return jnp.einsum("ai,ibc->abc", h_high, field, precision=lax.Precision.HIGHEST) * factor


def signs_low(table, h_low_half):
    return jnp.einsum("abj,jc->abc", table, h_low_half, preferred_element_type=jnp.float32)


def signs_mid(field, h_mid_half):
    return jnp.einsum("bj,ajc->abc", h_mid_half, field, preferred_element_type=jnp.float32)


def partner_gathered(spectrum, pair_list):
    mine = lax.axis_index("ao")
    mate = pair_list[mine]
    piece = lax.all_gather(spectrum[None], "ao", axis=0, tiled=True)
    start = jnp.int32(0)
    count = piece.shape[0]
    offset = jnp.clip(mate, 0, count - 1)
    chosen = lax.dynamic_index_in_dim(piece, offset, 0, keepdims=False)
    found = jnp.logical_and(mate >= start, mate < start + count)
    mates = jnp.where(found, chosen, jnp.zeros_like(spectrum))
    return spectrum * mates


def pair_product(spectrum, pair_list):
    return partner_gathered(spectrum, pair_list)


def body(truth_table, pair_list):
    table = truth_table[0]
    rows_here = table.shape[0]
    mid_len = table.shape[1]
    low_len = table.shape[2]
    high_len = rows_here * lax.axis_size("ma")
    factor = 1.0 / jnp.sqrt(jnp.float32(high_len * mid_len * low_len))
    h_high = sylvester(high_len)
    h_mid = sylvester(mid_len)
    h_low = sylvester(low_len)

    def high_step(field):
        return apply_high(field, h_high, factor)

    first_pass = signs_low(table, h_low.astype(jnp.bfloat16)).astype(jnp.bfloat16)
    partial_spec = signs_mid(first_pass, h_mid.astype(jnp.bfloat16))
    spectrum = high_step(
        lax.all_to_all(partial_spec, "ma", split_axis=1, concat_axis=0, tiled=True)
    )
    spectrum = lax.all_to_all(spectrum, "ma", split_axis=0, concat_axis=1, tiled=True)
    product = pair_product(spectrum, pair_list)
    product = apply_mid(apply_low(product, h_low), h_mid)
    mixed = high_step(lax.all_to_all(product, "ma", split_axis=1, concat_axis=0, tiled=True))
    result = lax.all_to_all(mixed, "ma", split_axis=0, concat_axis=1, tiled=True)
    return result[None]


def solution(mesh):
    return jax.shard_map(
        body,
        mesh=mesh,
        in_specs=(P("ao", "ma", None, None), P()),
        out_specs=P("ao", "ma", None, None),
        check_vma=False,
    )
```

profile of v0, /device:TPU:0, one launch (start us, length us, event | category | flops | bytes accessed | tf_op | source)
XLA Modules:
  0.0 2101.9 jit_solution(368012756062145836)
XLA Ops:
  6.5 0.0 all-gather.2.cloned.1.call-start
  6.5 13.9 convolution_bitcast_fusion.1
  20.4 16.6 copy.24
  37.0 370.1 %all_to_all.69 = f32[64,512,128]{2,0,1:T(8,128)S(1)} all-to-all(f32[64,512,128]{2,0,1:T(8,128)} %copy.24), channel_id=1, replica_groups=mesh['ma'=8,'ao'=4] {'ma'}, dimensions={1} | all-to-all | bytes 33554432 | tf_op jit(solution)/shard_map/all_to_all | solution.py:70
  407.1 1.7 copy.26
  408.9 32.3 %convolution_multiply_fusion.1 = f32[512,64,128]{2,0,1:T(8,128)S(1)} fusion(f32[512,64,128]{2,0,1:T(8,128)S(1)} %bitcast.58), kind=kOutput, calls=%fused_computation.5 | convolution fusion | flops 25784745984 | bytes 33554432 | tf_op jit(solution)/shard_map/ai,ibc->abc/dot_general | solution.py:25
  441.2 18.1 copy.27
  459.3 366.6 %all_to_all.70 = f32[512,64,128]{2,1,0:T(8,128)S(1)} all-to-all(f32[512,64,128]{2,1,0:T(8,128)S(1)} %copy.27), channel_id=1, replica_groups=mesh['ma'=8,'ao'=4] {'ma'}, dimensions={0} | all-to-all | bytes 33554432 | tf_op jit(solution)/shard_map/all_to_all | solution.py:72
  825.8 6.2 copy.28
  832.1 0.0 copy-start
  832.1 0.0 all-gather.2.cloned.1.call-update
  832.1 0.6 copy-done
  832.7 0.6 dynamic_slice.7
  835.2 388.0 %all-gather.2.cloned.1.call-done = f32[4,64,512,128]{3,2,1,0:T(8,128)} async-done(((f32[1,64,512,128]{3,2,1,0:T(8,128)}), f32[4,64,512,128]{3,2,1,0:T(8,128)}) %all-gather.2.cloned.1.call-update) | async-done | bytes 67108880 | tf_op jit(solution)/shard_map/all_gather | solution.py:39
  1223.3 24.5 %fusion = f32[64,512,128]{1,2,0:T(8,128)} fusion(f32[64,512,128]{2,1,0:T(8,128)} %bitcast.57, f32[4,64,512,128]{3,2,1,0:T(8,128)} %all-gather.2.cloned.1.call-done, s32[]{:T(128)} %bitcast.16, pred[]{:T(512)} %bitcast.13), kind=kOutput, calls=%fused_computation.1 | convolution fusion | flops 6451412992 | bytes 50332672 | tf_op jit(solution)/shard_map/abj,jc->abc/dot_general | solution.py:17
  1247.8 37.6 %convolution_bitcast_fusion = f32[64,512,128]{1,2,0:T(8,128)} fusion(f32[64,512,128]{1,2,0:T(8,128)} %fusion), kind=kOutput, calls=%fused_computation.6 | convolution fusion | flops 25780551680 | bytes 33554432 | tf_op jit(solution)/shard_map/bj,ajc->abc/dot_general | solution.py:21
  1285.4 16.6 copy.31
  1301.9 368.7 %all_to_all.71 = f32[64,512,128]{2,0,1:T(8,128)S(1)} all-to-all(f32[64,512,128]{2,0,1:T(8,128)} %copy.31), channel_id=1, replica_groups=mesh['ma'=8,'ao'=4] {'ma'}, dimensions={1} | all-to-all | bytes 33554432 | tf_op jit(solution)/shard_map/all_to_all | solution.py:75
  1670.6 1.7 copy.33
  1672.4 31.9 %convolution_multiply_fusion = f32[512,64,128]{2,0,1:T(8,128)S(1)} fusion(f32[512,64,128]{2,0,1:T(8,128)S(1)} %bitcast.59), kind=kOutput, calls=%fused_computation.4 | convolution fusion | flops 25784745984 | bytes 33554432 | tf_op jit(solution)/shard_map/ai,ibc->abc/dot_general | solution.py:25
  1704.3 18.1 copy.34
  1722.4 366.3 %all_to_all.72 = f32[512,64,128]{2,1,0:T(8,128)S(1)} all-to-all(f32[512,64,128]{2,1,0:T(8,128)S(1)} %copy.34), channel_id=1, replica_groups=mesh['ma'=8,'ao'=4] {'ma'}, dimensions={0} | all-to-all | bytes 33554432 | tf_op jit(solution)/shard_map/all_to_all | solution.py:76
  2088.6 6.2 copy.35
Async XLA Ops:
  6.5 1216.7 %all-gather.2.cloned.1.call-start = ((), (), s32[]{:S(2)}) async-start(), calls=%async_computation.4 | async-start | bytes 83886080 | tf_op jit(solution)/shard_map/all_gather | solution.py:39
  832.1 0.7 copy-start
Sparse Core Ops, SparseCore 0:
  832.2 391.0 all-gather.1
where the time goes:
time: 2110 us; the launch traced here: 2100 us
  blocking collectives  1470 us (70%)
  waiting for transfers between devices  388 us (18%)
  matrix products  140 us (7%)
  local copies, waits for them, and re-layouts  86.4 us (4%)
    all_gather x1, waiting for transfers between devices, partner_gathered(): piece = lax.all_gather(spectrum[None], 'ao', axis=0, tiled=True)  388 us
    all_to_all x1, blocking collectives, body(): lax.all_to_all(partial_spec, 'ma', split_axis=1, concat_axis=0, tiled=True)  370 us
    all_to_all x1, blocking collectives, body(): lax.all_to_all(product, 'ma', split_axis=1, concat_axis=0, tiled=True)  369 us
    all_to_all x1, blocking collectives, body(): lax.all_to_all(spectrum, 'ma', split_axis=0, concat_axis=1, tiled=True)  367 us
    all_to_all x1, blocking collectives, body(): lax.all_to_all(mixed, 'ma', split_axis=0, concat_axis=1, tiled=True)  366 us
    dot_general x2, matrix products, apply_high(): jnp.einsum('ai,ibc->abc', h_high, field, precision=lax.Precision.HIGHEST)  64.2 us
  transfers between devices with their start and end apart: 1, of which 1 were waited for; matrix products, arithmetic and copies ran while one was open for 0% of the time, Pallas kernels for 0%

commit v1 on v0

v1 whole, which is shorter than its diff:
```python
import jax
import jax.numpy as jnp
from jax import lax
from jax.sharding import PartitionSpec as P

BOTH = ("ma", "ao")


def sylvester(length):
    index_row = jnp.arange(length, dtype=jnp.int32)
    shared = jnp.bitwise_and(index_row[:, None], index_row[None, :])
    ones_count = jnp.zeros((length, length), jnp.int32)
    for position in range(length.bit_length() - 1):
        ones_count = ones_count + jnp.bitwise_and(jnp.right_shift(shared, position), 1)
    return (1 - 2 * (ones_count % 2)).astype(jnp.bfloat16)


def halves(field):
    upper = lax.reduce_precision(field, 8, 7)
    lower = field - upper
    return upper.astype(jnp.bfloat16), lower.astype(jnp.bfloat16)


def product_of(spec, field, h):
    upper, lower = halves(field)
    one = jnp.einsum(spec, h, upper, preferred_element_type=jnp.float32)
    return one + jnp.einsum(spec, h, lower, preferred_element_type=jnp.float32)


def body(truth_table, pair_list):
    table = truth_table[0]
    rows, mid, low = table.shape
    n_ma, n_ao = lax.axis_size("ma"), lax.axis_size("ao")
    devices = n_ma * n_ao
    high = rows * n_ma
    share = mid // devices
    factor = 1.0 / jnp.sqrt(jnp.float32(high * mid * low))
    h_high, h_mid, h_low = sylvester(high), sylvester(mid), sylvester(low)

    first = jnp.einsum("abj,jc->abc", table, h_low, preferred_element_type=jnp.float32)
    first = first.astype(jnp.bfloat16)
    h_parts = h_mid.reshape(devices, share, mid)
    partial = jnp.einsum("dbj,ajc->dabc", h_parts, first, preferred_element_type=jnp.float32)
    here = lax.all_to_all(partial, BOTH, split_axis=0, concat_axis=0, tiled=True)
    here = here.reshape(n_ma, n_ao, rows, share, low)
    here = here.transpose(1, 0, 2, 3, 4).reshape(n_ao, high, share * low)
    spectrum = product_of("hi,oir->ohr", here, h_high) * factor
    mates = jnp.stack(
        [
            lax.dynamic_index_in_dim(spectrum, pair_list[o], 0, keepdims=False)
            for o in range(n_ao)
        ]
    )
    product = spectrum * mates
    mixed = product_of("hi,oir->ohr", product, h_high) * factor
    mixed = mixed.reshape(n_ao, n_ma, rows * share, low)
    mixed = product_of("cj,omrj->omrc", mixed, h_low)
    mixed = mixed.reshape(n_ao, n_ma, rows, share, low).transpose(1, 0, 2, 3, 4)
    mixed = mixed.reshape(devices, rows, share, low)
    back = lax.all_to_all(mixed, BOTH, split_axis=0, concat_axis=0, tiled=True)
    h_parts = h_mid.reshape(mid, devices, share)
    return product_of("bdj,dajc->abc", back, h_parts)[None]


def solution(mesh):
    return jax.shard_map(
        body,
        mesh=mesh,
        in_specs=(P("ao", "ma", None, None), P()),
        out_specs=P("ao", "ma", None, None),
        check_vma=False,
    )
```

time: 2110 us -> 1080 us (0.51)
  blocking collectives: 1470 us -> 379 us
  matrix products: 140 us -> 186 us
  local copies, waits for them, and re-layouts: 86.4 us -> 131 us
  waiting for transfers between devices: 388 us -> 358 us
    all_to_all x4 -> x1, blocking collectives: 1470 us -> 379 us  [body(): back = lax.all_to_all(mixed, BOTH, split_axis=0, concat_axis=0, tiled=True)]
    all_gather x1 -> x0, waiting for transfers between devices: 388 us -> none  [partner_gathered(): piece = lax.all_gather(spectrum[None], 'ao', axis=0, tiled=True)]
    all_to_all x0 -> x1, waiting for transfers between devices: none -> 358 us  [body(): lax.all_to_all(partial, BOTH, split_axis=0, concat_axis=0, tiled=True)]
    reshape x0 -> x4, local copies, waits for them, and re-layouts: none -> 63.8 us  [the longest x2 34.3 us: body(): here = here.transpose(1, 0, 2, 3, 4).reshape(n_ao, high, share * low)]
    dot_general x5 -> x9, matrix products: 140 us -> 186 us  [the longest x4 93.9 us: product_of(): return one + jnp.einsum(spec, h, lower, preferred_element_type=jnp.float32)]
where the time goes in v1:
time: 1080 us; the launch traced here: 1070 us
  blocking collectives  379 us (35%)
  waiting for transfers between devices  358 us (33%)
  matrix products  186 us (17%)
  local copies, waits for them, and re-layouts  131 us (12%)
    all_to_all x1, blocking collectives, body(): back = lax.all_to_all(mixed, BOTH, split_axis=0, concat_axis=0, tiled=True)  379 us
    all_to_all x1, waiting for transfers between devices, body(): lax.all_to_all(partial, BOTH, split_axis=0, concat_axis=0, tiled=True)  358 us
    dot_general x4, matrix products, product_of(): return one + jnp.einsum(spec, h, lower, preferred_element_type=jnp.float32)  93.9 us
    dot_general x4, matrix products, product_of(): one = jnp.einsum(spec, h, upper, preferred_element_type=jnp.float32)  77 us
    reshape x2, local copies, waits for them, and re-layouts, body(): here = here.transpose(1, 0, 2, 3, 4).reshape(n_ao, high, share * low)  34.3 us
  transfers between devices with their start and end apart: 1, of which 1 were waited for; matrix products, arithmetic and copies ran while one was open for 0% of the time, Pallas kernels for 0%

profile of v1, /device:TPU:0, one launch (start us, length us, event | category | flops | bytes accessed | tf_op | source)
XLA Modules:
  0.0 1069.9 jit_solution(16449129503267911279)
XLA Ops:
  0.0 0.0 copy-start
  0.0 15.1 %convolution_bitcast_fusion = f32[32,64,16,128]{3,0,2,1:T(8,128)} fusion(bf16[1,64,512,128]{3,2,1,0:T(8,128)(2,1)} %param.2, s32[32,16]{0,1:T(8,128)S(1)} %multiply_add_fusion), kind=kOutput, calls=%fused_computation.18 | convolution fusion | flops 5384224768 | bytes 25167872 | tf_op jit(solution)/shard_map/dbj,ajc->dabc/dot_general | solution.py:43
  15.1 14.1 %copy.14 = f32[32,64,16,128]{3,2,1,0:T(8,128)} copy(f32[32,64,16,128]{3,0,2,1:T(8,128)} %convolution_bitcast_fusion) | data formatting | bytes 33554432 | tf_op jit(solution)/shard_map/dbj,ajc->dabc/transpose | solution.py:43
  29.2 0.0 copy-done
  29.2 0.0 copy-start.2
  29.2 7.9 all-to-all-start
  37.1 0.0 copy-done.2
  37.1 0.6 fusion.175
  44.8 358.0 %all-to-all-done = f32[32,64,16,128]{3,2,1,0:T(8,128)} async-done(((f32[32,64,16,128]{3,2,1,0:T(8,128)}), f32[32,64,16,128]{3,2,1,0:T(8,128)}, u32[]{:S(2)}, u32[]{:S(2)}) %all-to-all-start) | async-done | bytes 16777248 | tf_op jit(solution)/shard_map/all_to_all | solution.py:44
  402.8 11.5 %copy.36 = f32[8,4,64,16,128]{4,3,2,0,1:T(8,128)} copy(f32[8,4,64,16,128]{4,3,2,1,0:T(8,128)} %bitcast.6) | data formatting | bytes 33554432 | tf_op jit(solution)/shard_map/reshape | solution.py:45
  414.3 18.0 %reshape.42 = f32[4,512,2048]{2,1,0:T(8,128)} reshape(f32[4,8,64,16,128]{4,3,2,1,0:T(8,128)} %bitcast.85) | data formatting | bytes 33554432 | tf_op jit(solution)/shard_map/reshape | solution.py:46
  432.3 16.3 %copy.16 = f32[4,512,2048]{1,2,0:T(8,128)} copy(f32[4,512,2048]{2,1,0:T(8,128)} %reshape.42) | data formatting | bytes 33554432 | tf_op jit(solution)/shard_map/reshape | solution.py:46
  448.6 15.1 %fusion.11 = f32[4,2048,512]{2,1,0:T(8,128)} fusion(f32[4,512,2048]{1,2,0:T(8,128)} %copy.16), kind=kOutput, calls=%fused_computation.22 | convolution fusion | flops 4314103808 | bytes 33554432 | tf_op jit(solution)/shard_map/hi,oir->ohr/dot_general | solution.py:26
  463.7 17.6 %add_multiply_fusion = f32[4,2048,512]{2,1,0:T(8,128)} fusion(f32[4,2048,512]{2,1,0:T(8,128)} %fusion.11, f32[4,512,2048]{1,2,0:T(8,128)} %copy.16), kind=kOutput, calls=%fused_computation.17 | convolution fusion | flops 4326686720 | bytes 50331648 | tf_op jit(solution)/shard_map/hi,oir->ohr/dot_general | solution.py:27
  481.3 12.2 %dynamic-slice_bitcast_fusion.3 = (f32[1,512,2048]{1,2,0:T(8,128)}, f32[1,512,2048]{1,2,0:T(8,128)}, f32[1,512,2048]{1,2,0:T(8,128)}, f32[1,512,2048]{1,2,0:T(8,128)}) fusion(f32[4,2048,512]{2,1,0:T(8,128)} %add_multiply_fusion, s32[]{:T(128)S(6)} %select_n.49, s32[]{:T(128)S(6)} %select_n.52, s32[]{:T(128)S(6)} %select_n.51, s32[]{:T(128)S(6)} %select_n.50), kind=kLoop, calls=%fused_computation.33 | loop fusion | bytes 33554448 | tf_op jit(solution)/shard_map/jit(dynamic_index_in_dim)/dynamic_slice | solution.py:50
  493.5 18.8 %fusion.12 = f32[4,2048,512]{2,1,0:T(8,128)} fusion(f32[1,512,2048]{1,2,0:T(8,128)} %get-tuple-element.6, f32[1,512,2048]{1,2,0:T(8,128)} %get-tuple-element.7, f32[1,512,2048]{1,2,0:T(8,128)} %get-tuple-element.8, f32[1,512,2048]{1,2,0:T(8,128)} %get-tuple-element.5, f32[4,2048,512]{2,1,0:T(8,128)} %add_multiply_fusion), kind=kOutput, calls=%fused_computation.23 | convolution fusion | flops 4330881024 | bytes 50331648 | tf_op jit(solution)/shard_map/hi,oir->ohr/dot_general | solution.py:26
  512.2 25.2 %multiply_bitcast_fusion = f32[4,512,2048]{1,2,0:T(8,128)} fusion(f32[4,2048,512]{2,1,0:T(8,128)} %fusion.12, f32[1,512,2048]{1,2,0:T(8,128)} %get-tuple-element.6, f32[1,512,2048]{1,2,0:T(8,128)} %get-tuple-element.7, f32[1,512,2048]{1,2,0:T(8,128)} %get-tuple-element.8, f32[1,512,2048]{1,2,0:T(8,128)} %get-tuple-element.5, ...), kind=kOutput, calls=%fused_computation.16 | convolution fusion | flops 4343463936 | bytes 67108864 | tf_op jit(solution)/shard_map/hi,oir->ohr/dot_general | solution.py:27
  537.4 16.3 %copy.18 = f32[4,512,2048]{2,1,0:T(8,128)} copy(f32[4,512,2048]{1,2,0:T(8,128)} %multiply_bitcast_fusion) | data formatting | bytes 33554432 | tf_op jit(solution)/shard_map/mul | solution.py:55
  553.7 18.0 %reshape.43 = f32[4,8,1024,128]{3,2,1,0:T(8,128)} reshape(f32[4,512,2048]{2,1,0:T(8,128)} %copy.18) | data formatting | bytes 33554432 | tf_op jit(solution)/shard_map/reshape | solution.py:56
  571.7 13.9 %fusion.13 = f32[4,8,1024,128]{3,2,1,0:T(8,128)} fusion(f32[4,8,1024,128]{3,2,1,0:T(8,128)} %reshape.43), kind=kOutput, calls=%fused_computation.24 | convolution fusion | flops 1082703872 | bytes 33554432 | tf_op jit(solution)/shard_map/cj,omrj->omrc/dot_general | solution.py:26
  585.6 18.8 %convolution_add_fusion = f32[4,8,1024,128]{3,2,1,0:T(8,128)} fusion(f32[4,8,1024,128]{3,2,1,0:T(8,128)} %fusion.13, f32[4,8,1024,128]{3,2,1,0:T(8,128)} %reshape.43), kind=kOutput, calls=%fused_computation.19 | convolution fusion | flops 1091092480 | bytes 50331648 | tf_op jit(solution)/shard_map/cj,omrj->omrc/dot_general | solution.py:27
  604.4 6.7 copy.19
  611.1 0.0 copy-start.1
  611.1 379.4 %all_to_all.10 = f32[32,64,16,128]{3,2,1,0:T(8,128)} all-to-all(f32[32,64,16,128]{3,2,1,0:T(8,128)S(1)} %bitcast.86), channel_id=1, replica_groups=mesh['ma'=8,'ao'=4] {'ma','ao'}, dimensions={0} | all-to-all | bytes 33554432 | tf_op jit(solution)/shard_map/all_to_all | solution.py:60
  990.6 0.0 copy-done.1
  990.6 29.2 %fusion.14 = f32[64,128,512,1]{2,1,3,0:T(8,128)} fusion(f32[32,64,16,128]{3,2,1,0:T(8,128)} %all_to_all.10, s32[32,16]{0,1:T(8,128)S(1)} %copy-done.1), kind=kOutput, calls=%fused_computation.25 | convolution fusion | flops 4314103808 | bytes 33556480 | tf_op jit(solution)/shard_map/bdj,dajc->abc/dot_general | solution.py:26
  1019.8 32.4 %fusion.4 = f32[1,64,512,128]{2,3,1,0:T(8,128)} fusion(f32[64,128,512,1]{2,1,3,0:T(8,128)} %fusion.14, f32[32,64,16,128]{3,2,1,0:T(8,128)} %all_to_all.10, s32[32,16]{0,1:T(8,128)S(1)} %copy-done.1), kind=kOutput, calls=%fused_computation.14 | convolution fusion | flops 4322492416 | bytes 50333696 | tf_op jit(solution)/shard_map/bdj,dajc->abc/dot_general | solution.py:27
  1052.1 17.4 %copy.22 = f32[1,64,512,128]{3,2,1,0:T(8,128)} copy(f32[1,64,512,128]{2,3,1,0:T(8,128)} %fusion.4) | data formatting | bytes 33554432 | tf_op jit(solution)/shard_map/broadcast_in_dim | solution.py:62
  (1 shorter events, 0.0 us)
Async XLA Ops:
  0.0 29.2 %copy-start = (s32[32,16]{0,1:T(8,128)}, s32[32,16]{0,1:T(8,128)S(1)}, u32[]{:S(2)}) copy-start(s32[32,16]{0,1:T(8,128)S(1)} %multiply_add_fusion) | copy-start | bytes 6148
  29.2 7.9 copy-start.2
  29.2 373.6 %all-to-all-start = ((f32[32,64,16,128]{3,2,1,0:T(8,128)}), f32[32,64,16,128]{3,2,1,0:T(8,128)}, u32[]{:S(2)}, u32[]{:S(2)}) async-start(f32[32,64,16,128]{3,2,1,0:T(8,128)} %copy.14), calls=%async_computation | async-start | bytes 33554432 | tf_op jit(solution)/shard_map/all_to_all | solution.py:44
  611.1 379.5 %copy-start.1 = (s32[32,16]{0,1:T(8,128)S(1)}, s32[32,16]{0,1:T(8,128)}, u32[]{:S(2)}) copy-start(s32[32,16]{0,1:T(8,128)} %copy-done) | copy-start | bytes 6148

commit v2 on v1

v2 whole, which is shorter than its diff:
```python
import functools

import jax
import jax.numpy as jnp
from jax import lax
from jax.experimental import pallas as pl
from jax.experimental.pallas import tpu as pltpu
from jax.sharding import PartitionSpec as P

BOTH = ("ma", "ao")
VMEM_LIMIT = 56 * 1024 * 1024
CHUNKS = 1


def sylvester(length):
    index_row = jnp.arange(length, dtype=jnp.int32)
    shared = jnp.bitwise_and(index_row[:, None], index_row[None, :])
    ones_count = jnp.zeros((length, length), jnp.int32)
    for position in range(length.bit_length() - 1):
        ones_count = ones_count + jnp.bitwise_and(jnp.right_shift(shared, position), 1)
    return (1 - 2 * (ones_count % 2)).astype(jnp.bfloat16)


def halves(field):
    upper = field.astype(jnp.bfloat16)
    lower = (field - upper.astype(jnp.float32)).astype(jnp.bfloat16)
    return upper, lower


def dot(a, b):
    return jnp.dot(a, b, preferred_element_type=jnp.float32)


def left_product(h, field):
    upper, lower = halves(field)
    return dot(h, upper) + dot(h, lower)


def first_kernel(table_ref, mid_ref, low_ref, *out_refs):
    rows, mid, low = table_ref.shape
    devices, _, share, _ = out_refs[0].shape
    h_mid, h_low = mid_ref[...], low_ref[...]
    for a in range(0, rows, 2):
        pair = [dot(table_ref[a + k], h_low).astype(jnp.bfloat16) for k in range(2)]
        both = dot(h_mid, jnp.concatenate(pair, axis=1))
        for k in range(2):
            one = both[:, k * low:(k + 1) * low]
            one = one.reshape(devices, len(out_refs) * share, low)
            for c, out_ref in enumerate(out_refs):
                out_ref[:, a + k] = one[:, c * share:(c + 1) * share]


def middle_kernel(factor, pair_ref, in_ref, high_ref, low_ref, out_ref, spec_ref):
    n_ma, n_ao, rows, share, low = in_ref.shape
    high = n_ma * rows
    h_high = high_ref[...]
    h_low2 = jnp.concatenate([low_ref[...]] * 2, axis=0)
    for m in range(share):
        field = jnp.concatenate(
            [in_ref[:, o, :, m, :].reshape(high, low) for o in range(n_ao)], axis=1
        )
        spectrum = left_product(h_high, field) * factor
        for o in range(n_ao):
            spec_ref[o] = spectrum[:, o * low:(o + 1) * low]
        product = jnp.concatenate(
            [
                spec_ref[o] * spec_ref[jnp.clip(pair_ref[o], 0, n_ao - 1)]
                for o in range(n_ao)
            ],
            axis=1,
        )
        mixed = left_product(h_high, product) * factor
        for o in range(n_ao):
            parts = halves(mixed[:, o * low:(o + 1) * low])
            done = dot(jnp.concatenate(parts, axis=1), h_low2)
            out_ref[:, o, :, m, :] = done.reshape(n_ma, rows, low)


def last_kernel(mid_ref, *refs):
    *in_refs, out_ref = refs
    rows, mid, low = out_ref.shape
    h_mid = mid_ref[...]
    for a in range(0, rows, 2):
        pair = []
        for k in range(2):
            parts = [ref[:, a + k] for ref in in_refs]
            one = parts[0] if len(parts) == 1 else jnp.concatenate(parts, axis=1)
            pair.append(one.reshape(mid, low))
        both = left_product(h_mid, jnp.concatenate(pair, axis=1))
        for k in range(2):
            out_ref[a + k] = both[:, k * low:(k + 1) * low]


def params():
    return pltpu.CompilerParams(vmem_limit_bytes=VMEM_LIMIT)


def whole(array):
    return pl.BlockSpec(array.shape, lambda i: (0,) * array.ndim)


def body(truth_table, pair_list):
    table = truth_table[0]
    rows, mid, low = table.shape
    n_ma, n_ao = lax.axis_size("ma"), lax.axis_size("ao")
    devices = n_ma * n_ao
    high = rows * n_ma
    share = mid // devices
    chunks = CHUNKS if share % (8 * CHUNKS) == 0 else 1
    part = share // chunks
    step = min(8, rows)
    block = min(8, part)
    factor = float(1.0 / (high * mid * low) ** 0.5)
    h_high, h_mid, h_low = sylvester(high), sylvester(mid), sylvester(low)
    sent = jax.ShapeDtypeStruct((devices, rows, part, low), jnp.float32)
    rows_spec = pl.BlockSpec((devices, step, part, low), lambda i: (0, i, 0, 0))
    table_spec = pl.BlockSpec((step, mid, low), lambda i: (i, 0, 0))

    partial = pl.pallas_call(
        first_kernel,
        grid=(rows // step,),
        in_specs=[table_spec, whole(h_mid), whole(h_low)],
        out_specs=[rows_spec] * chunks,
        out_shape=[sent] * chunks,
        compiler_params=params(),
        cost_estimate=pl.CostEstimate(
            flops=2 * rows * mid * low * (mid + low),
            bytes_accessed=6 * rows * mid * low,
            transcendentals=0,
        ),
    )(table, h_mid, h_low)

    five = (n_ma, n_ao, rows, part, low)
    five_spec = pl.BlockSpec((n_ma, n_ao, rows, block, low), lambda i: (0, 0, 0, i, 0))
    middle = pl.pallas_call(
        functools.partial(middle_kernel, factor),
        grid=(part // block,),
        in_specs=[
            pl.BlockSpec(memory_space=pltpu.SMEM),
            five_spec,
            whole(h_high),
            whole(h_low),
        ],
        out_specs=five_spec,
        out_shape=jax.ShapeDtypeStruct(five, jnp.float32),
        scratch_shapes=[pltpu.VMEM((n_ao, high, low), jnp.float32)],
        compiler_params=params(),
        cost_estimate=pl.CostEstimate(
            flops=8 * n_ao * high * part * low * high,
            bytes_accessed=8 * n_ao * high * part * low,
            transcendentals=0,
        ),
    )

    back = []
    for piece in partial:
        here = lax.all_to_all(piece, BOTH, split_axis=0, concat_axis=0, tiled=True)
        mixed = middle(pair_list, here.reshape(five), h_high, h_low)
        mixed = mixed.reshape(devices, rows, part, low)
        back.append(lax.all_to_all(mixed, BOTH, split_axis=0, concat_axis=0, tiled=True))

    result = pl.pallas_call(
        last_kernel,
        grid=(rows // step,),
        in_specs=[whole(h_mid)] + [rows_spec] * chunks,
        out_specs=table_spec,
        out_shape=jax.ShapeDtypeStruct((rows, mid, low), jnp.float32),
        compiler_params=params(),
        cost_estimate=pl.CostEstimate(
            flops=4 * rows * mid * low * mid,
            bytes_accessed=8 * rows * mid * low,
            transcendentals=0,
        ),
    )(h_mid, *back)
    return result[None]


def solution(mesh):
    return jax.shard_map(
        body,
        mesh=mesh,
        in_specs=(P("ao", "ma", None, None), P()),
        out_specs=P("ao", "ma", None, None),
        check_vma=False,
    )
```

time: 1080 us -> 821 us (0.76)
  blocking collectives: 379 us -> 738 us
  waiting for transfers between devices: 358 us -> 0 us
  matrix products: 186 us -> 0 us
  local copies, waits for them, and re-layouts: 131 us -> 0 us
  Pallas kernels: 0 us -> 79.8 us
    all_to_all x1 -> x2, blocking collectives: 379 us -> 738 us  [the longest x1 371 us: body(): here = lax.all_to_all(piece, BOTH, split_axis=0, concat_axis=0, tiled=True)]
    all_to_all x1 -> x0, waiting for transfers between devices: 358 us -> none  [body(): lax.all_to_all(partial, BOTH, split_axis=0, concat_axis=0, tiled=True)]
    dot_general x9 -> x0, matrix products: 186 us -> none  [the longest x4 93.9 us: product_of(): return one + jnp.einsum(spec, h, lower, preferred_element_type=jnp.float32)]
    pallas_call x0 -> x3, Pallas kernels: none -> 79.8 us  [the longest x1 47.9 us: body(): mixed = middle(pair_list, here.reshape(five), h_high, h_low)]
    reshape x4 -> x0, local copies, waits for them, and re-layouts: 63.8 us -> none  [the longest x2 34.3 us: body(): here = here.transpose(1, 0, 2, 3, 4).reshape(n_ao, high, share * low)]
    transpose x2 -> x0, local copies, waits for them, and re-layouts: 20.8 us -> none  [the longest x1 14.1 us: body(): jnp.einsum('dbj,ajc->dabc', h_parts, first, preferred_element_type=jnp.fl...]
    broadcast_in_dim x1 -> x0, local copies, waits for them, and re-layouts: 17.4 us -> none  [body(): return product_of('bdj,dajc->abc', back, h_parts)[None]]
    mul x1 -> x0, local copies, waits for them, and re-layouts: 16.3 us -> none  [body(): mixed = product_of('hi,oir->ohr', product, h_high) * factor]
  transfers between devices with their start and end apart: 1 -> 0, of which waited for: 1 -> 0; matrix products, arithmetic and copies ran while one was open for 0% -> 0% of each run, Pallas kernels for 0% -> 0%
where the time goes in v2:
time: 821 us
  blocking collectives  738 us (90%)
  Pallas kernels  79.8 us (10%)
    all_to_all x1, blocking collectives, body(): here = lax.all_to_all(piece, BOTH, split_axis=0, concat_axis=0, tiled=True)  371 us
    all_to_all x1, blocking collectives, body(): lax.all_to_all(mixed, BOTH, split_axis=0, concat_axis=0, tiled=True)  367 us
    pallas_call x1, Pallas kernels, body(): mixed = middle(pair_list, here.reshape(five), h_high, h_low)  47.9 us
    pallas_call x1, Pallas kernels, body(): pl.pallas_call(last_kernel, grid=(rows // step,), in_specs=[whole(h_mid)]...  17.2 us

profile of v2, /device:TPU:0, one launch (start us, length us, event | category | flops | bytes accessed | tf_op | source)
XLA Modules:
  0.0 820.9 jit_solution(11875435525342809441)
XLA Ops:
  0.0 0.7 fusion.7.low_ref
  0.7 2.2 fusion.3.mid_ref.high_ref
  2.9 14.8 %shard_map.28 = f32[32,64,16,128]{3,2,1,0:T(8,128)} custom-call(bf16[64,512,128]{2,1,0:T(8,128)(2,1)} %bitcast.6, bf16[512,512]{1,0:T(8,128)(2,1)} %fusion.3.mid_ref.high_ref, bf16[128,128]{1,0:T(8,128)(2,1)} %fusion.7.low_ref), custom_call_target="tpu_custom_call" | custom-call | flops 5368709120 | bytes 25165824 | tf_op jit(solution)/shard_map/pallas_call | solution.py:119
  17.7 370.7 %all_to_all.10 = f32[32,64,16,128]{3,2,1,0:T(8,128)} all-to-all(f32[32,64,16,128]{3,2,1,0:T(8,128)} %shard_map.28), channel_id=1, replica_groups=mesh['ma'=8,'ao'=4] {'ma','ao'}, dimensions={0} | all-to-all | bytes 33554432 | tf_op jit(solution)/shard_map/all_to_all | solution.py:157
  388.4 47.9 %shard_map.29 = f32[8,4,64,16,128]{4,3,2,1,0:T(8,128)} custom-call(s32[4]{0:T(128)} %pair_ref.1, f32[8,4,64,16,128]{4,3,2,1,0:T(8,128)} %bitcast.4, bf16[512,512]{1,0:T(8,128)(2,1)} %fusion.3.mid_ref.high_ref, bf16[128,128]{1,0:T(8,128)(2,1)} %fusion.7.low_ref), custom_call_target="tpu_custom_call" | custom-call | flops 17179869184 | bytes 33554432 | tf_op jit(solution)/shard_map/pallas_call | solution.py:158
  436.3 367.5 %all_to_all.11.refs_0_ = f32[32,64,16,128]{3,2,1,0:T(8,128)} all-to-all(f32[32,64,16,128]{3,2,1,0:T(8,128)} %bitcast.5), channel_id=1, replica_groups=mesh['ma'=8,'ao'=4] {'ma','ao'}, dimensions={0} | all-to-all | bytes 33554432 | tf_op jit(solution)/shard_map/all_to_all | solution.py:160
  803.7 17.2 %shard_map.30 = f32[64,512,128]{2,1,0:T(8,128)} custom-call(bf16[512,512]{1,0:T(8,128)(2,1)} %fusion.3.mid_ref.high_ref, f32[32,64,16,128]{3,2,1,0:T(8,128)} %all_to_all.11.refs_0_), custom_call_target="tpu_custom_call" | custom-call | flops 8589934592 | bytes 33554432 | tf_op jit(solution)/shard_map/pallas_call | solution.py:162

commit v3 on v2

--- a/solution.py
+++ b/solution.py
@@ -9,7 +9,7 @@
 
 BOTH = ("ma", "ao")
 VMEM_LIMIT = 56 * 1024 * 1024
-CHUNKS = 1
+CHUNKS = 2
 
 
 def sylvester(length):

time: 821 us -> 802 us (0.977)
  blocking collectives: 738 us -> 382 us
  waiting for transfers between devices: 0 us -> 315 us
  starting transfers between devices: 0 us -> 11.6 us
    all_to_all x0 -> x2, waiting for transfers between devices: none -> 315 us  [the longest x1 158 us: body(): lax.all_to_all(mixed, BOTH, split_axis=0, concat_axis=0, tiled=True)]
    all_to_all x1, blocking collectives: 371 us -> 191 us  [body(): here = lax.all_to_all(piece, BOTH, split_axis=0, concat_axis=0, tiled=True)]
    all_to_all x1, blocking collectives: 367 us -> 191 us  [body(): lax.all_to_all(mixed, BOTH, split_axis=0, concat_axis=0, tiled=True)]
    all_to_all x0 -> x2, starting transfers between devices: none -> 11.6 us  [the longest x1 7.44 us: body(): lax.all_to_all(mixed, BOTH, split_axis=0, concat_axis=0, tiled=True)]
    pallas_call x1 -> x2, Pallas kernels: 47.9 us -> 55.2 us  [body(): mixed = middle(pair_list, here.reshape(five), h_high, h_low)]
  transfers between devices with their start and end apart: 0 -> 2, of which waited for: 0 -> 2; matrix products, arithmetic and copies ran while one was open for 0% -> 0% of each run, Pallas kernels for 0% -> 7%
where the time goes in v3:
time: 802 us; the launch traced here: 799 us
  blocking collectives  382 us (48%)
  waiting for transfers between devices  315 us (39%)
  Pallas kernels  87 us (11%)
  starting transfers between devices  11.6 us (1%)
    all_to_all x1, blocking collectives, body(): lax.all_to_all(mixed, BOTH, split_axis=0, concat_axis=0, tiled=True)  191 us
    all_to_all x1, blocking collectives, body(): here = lax.all_to_all(piece, BOTH, split_axis=0, concat_axis=0, tiled=True)  191 us
    all_to_all x1, waiting for transfers between devices, body(): lax.all_to_all(mixed, BOTH, split_axis=0, concat_axis=0, tiled=True)  158 us
    all_to_all x1, waiting for transfers between devices, body(): here = lax.all_to_all(piece, BOTH, split_axis=0, concat_axis=0, tiled=True)  157 us
    pallas_call x2, Pallas kernels, body(): mixed = middle(pair_list, here.reshape(five), h_high, h_low)  55.2 us
    pallas_call x1, Pallas kernels, body(): pl.pallas_call(last_kernel, grid=(rows // step,), in_specs=[whole(h_mid)]...  17 us
  transfers between devices with their start and end apart: 2, of which 2 were waited for; matrix products, arithmetic and copies ran while one was open for 0% of the time, Pallas kernels for 7%

profile of v3, /device:TPU:0, one launch (start us, length us, event | category | flops | bytes accessed | tf_op | source)
XLA Modules:
  0.0 798.9 jit_solution(6296810242428448406)
XLA Ops:
  0.0 0.7 fusion.7.low_ref
  0.7 2.3 fusion.3.mid_ref.high_ref
  3.0 14.8 %shard_map.28 = (f32[32,64,8,128]{3,2,1,0:T(8,128)}, f32[32,64,8,128]{3,2,1,0:T(8,128)}) custom-call(bf16[64,512,128]{2,1,0:T(8,128)(2,1)} %bitcast.9, bf16[512,512]{1,0:T(8,128)(2,1)} %fusion.3.mid_ref.high_ref, bf16[128,128]{1,0:T(8,128)(2,1)} %fusion.7.low_ref), custom_call_target="tpu_custom_call" | custom-call | flops 5368709120 | bytes 25165824 | tf_op jit(solution)/shard_map/pallas_call | solution.py:119
  17.8 190.9 %all_to_all.20 = f32[32,64,8,128]{3,2,1,0:T(8,128)} all-to-all(f32[32,64,8,128]{3,2,1,0:T(8,128)} %get-tuple-element.7), channel_id=1, replica_groups=mesh['ma'=8,'ao'=4] {'ma','ao'}, dimensions={0} | all-to-all | bytes 16777216 | tf_op jit(solution)/shard_map/all_to_all | solution.py:157
  208.8 4.1 all-to-all-start.2
  212.9 27.8 %shard_map.29 = f32[8,4,64,8,128]{4,3,2,1,0:T(8,128)} custom-call(s32[4]{0:T(128)} %pair_ref.3, f32[8,4,64,8,128]{4,3,2,1,0:T(8,128)} %bitcast.7, bf16[512,512]{1,0:T(8,128)(2,1)} %fusion.3.mid_ref.high_ref, bf16[128,128]{1,0:T(8,128)(2,1)} %fusion.7.low_ref), custom_call_target="tpu_custom_call" | custom-call | flops 8589934592 | bytes 16777216 | tf_op jit(solution)/shard_map/pallas_call | solution.py:158
  240.7 157.3 %all-to-all-done.2 = f32[32,64,8,128]{3,2,1,0:T(8,128)} async-done(((f32[32,64,8,128]{3,2,1,0:T(8,128)}), f32[32,64,8,128]{3,2,1,0:T(8,128)}, u32[]{:S(2)}, u32[]{:S(2)}) %all-to-all-start.2) | async-done | bytes 8388640 | tf_op jit(solution)/shard_map/all_to_all | solution.py:157
  398.0 7.4 all-to-all-start.1
  405.5 27.4 %shard_map.30 = f32[8,4,64,8,128]{4,3,2,1,0:T(8,128)} custom-call(s32[4]{0:T(128)} %pair_ref.3, f32[8,4,64,8,128]{4,3,2,1,0:T(8,128)} %bitcast.3.in_ref, bf16[512,512]{1,0:T(8,128)(2,1)} %fusion.3.mid_ref.high_ref, bf16[128,128]{1,0:T(8,128)(2,1)} %fusion.7.low_ref), custom_call_target="tpu_custom_call" | custom-call | flops 8589934592 | bytes 16777216 | tf_op jit(solution)/shard_map/pallas_call | solution.py:158
  432.8 157.9 %all-to-all-done.1.refs_0_ = f32[32,64,8,128]{3,2,1,0:T(8,128)} async-done(((f32[32,64,8,128]{3,2,1,0:T(8,128)}), f32[32,64,8,128]{3,2,1,0:T(8,128)}, u32[]{:S(2)}, u32[]{:S(2)}) %all-to-all-start.1) | async-done | bytes 8388640 | tf_op jit(solution)/shard_map/all_to_all | solution.py:160
  590.7 191.0 %all_to_all.21.refs_1_ = f32[32,64,8,128]{3,2,1,0:T(8,128)} all-to-all(f32[32,64,8,128]{3,2,1,0:T(8,128)} %bitcast.8), channel_id=1, replica_groups=mesh['ma'=8,'ao'=4] {'ma','ao'}, dimensions={0} | all-to-all | bytes 16777216 | tf_op jit(solution)/shard_map/all_to_all | solution.py:160
  781.7 17.0 %shard_map.31 = f32[64,512,128]{2,1,0:T(8,128)} custom-call(bf16[512,512]{1,0:T(8,128)(2,1)} %fusion.3.mid_ref.high_ref, f32[32,64,8,128]{3,2,1,0:T(8,128)} %all-to-all-done.1.refs_0_, f32[32,64,8,128]{3,2,1,0:T(8,128)} %all_to_all.21.refs_1_), custom_call_target="tpu_custom_call" | custom-call | flops 8589934592 | bytes 33554432 | tf_op jit(solution)/shard_map/pallas_call | solution.py:162
Async XLA Ops:
  208.8 189.2 %all-to-all-start.2 = ((f32[32,64,8,128]{3,2,1,0:T(8,128)}), f32[32,64,8,128]{3,2,1,0:T(8,128)}, u32[]{:S(2)}, u32[]{:S(2)}) async-start(f32[32,64,8,128]{3,2,1,0:T(8,128)} %get-tuple-element.8), calls=%async_computation.2 | async-start | bytes 16777216 | tf_op jit(solution)/shard_map/all_to_all | solution.py:157
  398.0 192.7 %all-to-all-start.1 = ((f32[32,64,8,128]{3,2,1,0:T(8,128)}), f32[32,64,8,128]{3,2,1,0:T(8,128)}, u32[]{:S(2)}, u32[]{:S(2)}) async-start(f32[32,64,8,128]{3,2,1,0:T(8,128)} %bitcast.6), calls=%async_computation.1 | async-start | bytes 16777216 | tf_op jit(solution)/shard_map/all_to_all | solution.py:160
